TPU v7x, 32 devices: a whole 2x2x4 slice. The times are simulated.
32 devices in a mesh: grp: 2 (over y), user: 4 (over z), blk: 2 (over x), sub: 2 (over core).
Axes of the slice: x: 2, y: 2, z: 4, core: 2. Of those that a mesh axis runs over, the one named last changes fastest.
Arguments:
- engagement: bfloat16 [24576, 512], P(('grp', 'blk', 'sub'), 'user'), parts along dimension 0, may hold values from -6 to 6
- pattern: int32 [192, 4], P(('grp', 'blk', 'sub')), parts along dimension 0, may hold values 0 or 1
- degree: int32 [24576], P(('grp', 'blk', 'sub')), parts along dimension 0, may hold values from 1 to 256
Outputs:
- cooccur: float32 [1024, 512], P(('grp', 'user'), ('blk', 'sub')), parts along dimension 0
There are 2 independent parts, one for each index of `grp`. A program takes and returns all parts, laid end to end along the dimension named above; each array names one. Nothing has to cross between parts.
All inputs are finite; a program needn't handle non-finite values. No bound on the sum of `pattern` on one device may be relied on, other than what follows from the above.
Results may differ from a plain program's by a relative error of at most 0.00097.
Values may be sent and summed in bfloat16 or wider, within the bound.
A program may use at most 64 MiB of HBM per device.

v0:
```python
import jax
import jax.numpy as jnp
from jax import lax
from jax.sharding import PartitionSpec as P


def contract(first, second):
    return lax.dot_general(
        first, second, (((0,), (0,)), ((), ())), preferred_element_type=jnp.float32
    )


def on_device(engagement, pattern, degree):
    own_block = lax.axis_index("user")
    user_rows = engagement.shape[0]
    width = engagement.shape[1]
    tiles = pattern.shape[0]
    n_blk = lax.axis_size("blk")
    n_sub = lax.axis_size("sub")
    n_user = lax.axis_size("user")
    total_users = user_rows * n_blk * n_sub
    column_mask = lax.dynamic_slice_in_dim(pattern, own_block, 1, 1).astype(jnp.bfloat16)
    masked = (
        engagement.reshape(tiles, user_rows // tiles, width) * column_mask[:, :, None]
    ).reshape(user_rows, width)
    weight = jnp.sqrt(lax.rsqrt(degree.astype(jnp.float32))) * float(total_users) ** (-0.25)
    left = (masked.astype(jnp.float32) * weight[:, None]).astype(jnp.bfloat16)
    items = width * n_user
    partial_rows = contract(left, lax.all_gather(left, "user", axis=1, tiled=True))
    column_block = jnp.arange(items, dtype=jnp.int32) // width
    partial_rows = jnp.where(column_block[None, :] >= own_block, partial_rows, jnp.float32(0.0))
    result = lax.psum_scatter(partial_rows, ("blk", "sub"), scatter_dimension=1, tiled=True)
    return result


def solution(mesh):
    placed = (
        P(("grp", "blk", "sub"), "user"),
        P(("grp", "blk", "sub"), None),
        P(("grp", "blk", "sub")),
    )
    return jax.shard_map(
        on_device,
        mesh=mesh,
        in_specs=placed,
        out_specs=P(("grp", "user"), ("blk", "sub")),
        check_vma=False,
    )
```

profile of v0, /device:TPU:1, one launch (start us, length us, event | category | flops | bytes accessed | tf_op | source)
XLA Modules:
  0.0 106.0 jit_solution(15273683021830793084)
XLA Ops:
  6.5 0.0 all-gather.2.cloned.1.call-start
  6.5 0.7 convert_bitcast_fusion
  7.2 0.1 broadcast_bitcast_fusion
  7.3 0.7 sqrt_multiply_fusion
  8.0 3.7 %multiply_convert_fusion = bf16[3072,128]{1,0:T(8,128)(2,1)} fusion(f32[3072]{0:T(1024)S(1)} %sqrt_multiply_fusion, bf16[3072,128]{1,0:T(8,128)(2,1)} %param.3, bf16[3072]{0:T(1024)(128)(2,1)S(1)} %broadcast_bitcast_fusion), kind=kLoop, calls=%fused_computation | loop fusion | flops 1572864 | bytes 1591296 | tf_op jit(solution)/shard_map/convert_element_type | solution.py:27
  11.7 0.0 all-gather.2.cloned.1.call-update
  11.7 0.0 reduce-scatter.2.cloned.1.call-start
  11.8 65.7 %all-gather.2.cloned.1.call-done = bf16[3072,512]{1,0:T(8,128)(2,1)} async-done(((bf16[3072,128]{1,0:T(8,128)(2,1)}), bf16[3072,512]{1,0:T(8,128)(2,1)}) %all-gather.2.cloned.1.call-update) | async-done | bytes 3145744 | tf_op jit(solution)/shard_map/all_gather | solution.py:29
  77.5 3.5 %convolution_select_fusion = f32[128,512]{1,0:T(8,128)} fusion(bf16[3072,128]{1,0:T(8,128)(2,1)} %multiply_convert_fusion, bf16[3072,512]{1,0:T(8,128)(2,1)} %all-gather.2.cloned.1.call-done, pred[512]{0:T(512)(128)(4,1)S(1)} %fusion), kind=kOutput, calls=%fused_computation.1 | convolution fusion | flops 402718720 | bytes 4194816 | tf_op jit(solution)/shard_map/dot_general | solution.py:8
  81.0 0.0 reduce-scatter.2.cloned.1.call-update
  81.0 18.2 %reduce-scatter.2.cloned.1.call-done = f32[128,128]{1,0:T(8,128)} async-done(((f32[128,512]{1,0:T(8,128)}), f32[128,128]{1,0:T(8,128)}) %reduce-scatter.2.cloned.1.call-update) | async-done | bytes 65552 | tf_op jit(solution)/shard_map/reduce_scatter | solution.py:32
  (1 shorter events, 0.0 us)
Async XLA Ops:
  6.5 71.0 %all-gather.2.cloned.1.call-start = ((), (), s32[]{:S(2)}) async-start(), calls=%async_computation.1 | async-start | bytes 3932160 | tf_op jit(solution)/shard_map/all_gather | solution.py:29
  11.7 87.5 %reduce-scatter.2.cloned.1.call-start = ((), (), s32[]{:S(2)}) async-start(), calls=%async_computation.2 | async-start | bytes 327680 | tf_op jit(solution)/shard_map/reduce_scatter | solution.py:32
Sparse Core Ops, SparseCore 0:
  11.8 65.6 all-gather.1
  81.1 18.0 reduce-scatter.1
where the time goes:
time: 107 us; the launch traced here: 106 us
  waiting for transfers between devices  83.9 us (78%)
  between operations  13.4 us (13%)
  other arithmetic  5.09 us (5%)
  matrix products  3.46 us (3%)
    all_gather x1, waiting for transfers between devices, on_device(): lax.all_gather(left, 'user', axis=1, tiled=True)  65.7 us
    reduce_scatter x1, waiting for transfers between devices, on_device(): lax.psum_scatter(partial_rows, ('blk', 'sub'), scatter_dimension=1, tiled...  18.2 us
    convert_element_type x1, other arithmetic, on_device(): left = (masked.astype(jnp.float32) * weight[:, None]).astype(jnp.bfloat16)  3.67 us
    dot_general x1, matrix products, contract(): lax.dot_general(first, second, (((0,), (0,)), ((), ())), preferred_elemen...  3.46 us
  transfers between devices with their start and end apart: 2, of which 2 were waited for; matrix products, arithmetic and copies ran while one was open for 0% of the time, Pallas kernels for 0%

commit v1 on v0

v1 whole, which is shorter than its diff:
```python
import functools

import jax
import jax.numpy as jnp
from jax import lax
from jax.experimental import pallas as pl
from jax.experimental.pallas import tpu as pltpu
from jax.sharding import PartitionSpec as P

MESH = pl.DeviceIdType.MESH


def contract(first, second):
    return lax.dot_general(
        first, second, (((0,), (0,)), ((), ())), preferred_element_type=jnp.float32
    )


def pair_slot(n, i, j):
    return i * n - (i * (i + 1)) // 2 + (j - i - 1)


def kernel(
    n, nb, ns, chunks, eng_hbm, pattern_ref, degree_ref, out_ref,
    eng, left, acc, other, diag, landed,
    load_sem, in_send, in_recv, core_send, core_recv, out_send, out_recv, diag_send,
):
    g, z = lax.axis_index("grp"), lax.axis_index("user")
    x, c = lax.axis_index("blk"), lax.axis_index("sub")
    rows, width = eng.shape
    tiles = degree_ref.shape[0]
    tile = rows // tiles
    half = rows // 2
    step = half // chunks
    procs = (n // 2 - 1, n // 2)
    column = x * ns + c
    pairs = [(i, j) for i in range(n) for j in range(i + 1, n)]

    load = pltpu.make_async_copy(eng_hbm, eng, load_sem)
    load.start()

    barrier = pltpu.get_barrier_semaphore()
    everyone = n * nb * ns

    def greet(k, carry):
        zz, xx, cc = k // (nb * ns), (k // ns) % nb, k % ns

        @pl.when((zz != z) | (xx != x) | (cc != c))
        def _():
            pl.semaphore_signal(barrier, inc=1, device_id=(g, zz, xx, cc), device_id_type=MESH)

        return carry

    lax.fori_loop(0, everyone, greet, 0)

    lanes = lax.broadcasted_iota(jnp.int32, pattern_ref.shape, 1)
    mask = jnp.sum(jnp.where(lanes == z, pattern_ref[...], 0), axis=1, keepdims=True)
    weight = jnp.sqrt(lax.rsqrt(degree_ref[...].astype(jnp.float32)))
    weight = weight * float(rows * nb * ns) ** (-0.25) * mask.astype(jnp.float32)
    weight = weight.T

    load.wait()

    def prepare(p, k):
        start = p * half + k * step
        for t in range(start // tile, (start + step) // tile):
            at = pl.ds(t * tile, tile)
            scaled = eng[at, :].astype(jnp.float32) * weight[:, t : t + 1]
            left[z, at, :] = scaled.astype(jnp.bfloat16)

    def block_copy(source, p, k):
        at = pl.ds(p * half + k * step, step)
        return pltpu.make_async_remote_copy(
            src_ref=left.at[source, at, :],
            dst_ref=left.at[source, at, :],
            send_sem=in_send.at[p, k],
            recv_sem=in_recv.at[source, k],
            device_id=(g, procs[p] if isinstance(p, int) else procs[0] + p, x, c),
            device_id_type=MESH,
        )

    for k in range(chunks):
        for p in range(2):
            prepare(p, k)
        if k == 0:
            pl.semaphore_wait(barrier, everyone - 1)
        for p in range(2):

            @pl.when(z != procs[p])
            def _():
                block_copy(z, p, k).start()

    def diag_copy(slot):
        return pltpu.make_async_remote_copy(
            src_ref=diag,
            dst_ref=landed.at[slot],
            send_sem=diag_send,
            recv_sem=out_recv.at[slot],
            device_id=(g, z, z // ns, lax.rem(z, ns)),
            device_id_type=MESH,
        )

    diag[...] = contract(left[z], left[z])

    @pl.when(column != z)
    def _():
        diag_copy(c * nb + x).start()

    def core_copy(s):
        return pltpu.make_async_remote_copy(
            src_ref=acc.at[s],
            dst_ref=other.at[s],
            send_sem=core_send.at[s],
            recv_sem=core_recv.at[s],
            device_id=(g, z, x, 1 - c),
            device_id_type=MESH,
        )

    def out_copy(s, slot, i, j):
        return pltpu.make_async_remote_copy(
            src_ref=acc.at[s],
            dst_ref=landed.at[slot],
            send_sem=out_send.at[s],
            recv_sem=out_recv.at[slot],
            device_id=(g, i, j // ns, c),
            device_id_type=MESH,
        )

    is_proc = (z == procs[0]) | (z == procs[1])

    @pl.when(is_proc)
    def _():
        p = z - procs[0]
        acc[...] = jnp.zeros_like(acc)

        def multiply(k, carry):
            for i in range(n):

                @pl.when(z != i)
                def _():
                    block_copy(i, p, k).wait_recv()

            at = pl.ds(pl.multiple_of(p * half + k * step, 16), step)
            for s, (i, j) in enumerate(pairs):
                acc[s] += contract(left[i, at, :], left[j, at, :])
            return carry

        lax.fori_loop(0, chunks, multiply, 0)

        for s, (i, j) in enumerate(pairs):

            @pl.when(c != j % ns)
            def _():
                core_copy(s).start()

        for s, (i, j) in enumerate(pairs):

            @pl.when(c == j % ns)
            def _():
                core_copy(s).wait_recv()
                acc[s] += other[s]

                @pl.when((z != i) | (x != j // ns))
                def _():
                    out_copy(s, p * nb + x, i, j).start()

    @pl.when(column < z)
    def _():
        out_ref[...] = jnp.zeros_like(out_ref)

    @pl.when(column == z)
    def _():
        out_ref[...] = diag[...]
        for cc in range(ns):
            for xx in range(nb):

                @pl.when((xx != x) | (cc != c))
                def _():
                    slot = cc * nb + xx
                    diag_copy(slot).wait_recv()
                    out_ref[...] += landed[slot]

    @pl.when(column > z)
    def _():
        out_ref[...] = jnp.zeros_like(out_ref)

        @pl.when(is_proc)
        def _():
            out_ref[...] = acc[pair_slot(n, z, column)]

        for p in range(2):
            for xx in range(nb):

                @pl.when((z != procs[p]) | (xx != x))
                def _():
                    slot = p * nb + xx
                    out_copy(0, slot, z, column).wait_recv()
                    out_ref[...] += landed[slot]

    for k in range(chunks):
        for p in range(2):

            @pl.when(z != procs[p])
            def _():
                block_copy(z, p, k).wait_send()

    @pl.when(column != z)
    def _():
        diag_copy(0).wait_send()

    @pl.when(is_proc)
    def _():
        for s, (i, j) in enumerate(pairs):

            @pl.when(c != j % ns)
            def _():
                core_copy(s).wait_send()

            @pl.when((c == j % ns) & ((z != i) | (x != j // ns)))
            def _():
                out_copy(s, 0, i, j).wait_send()


def on_device(engagement, pattern, degree):
    n, nb, ns = lax.axis_size("user"), lax.axis_size("blk"), lax.axis_size("sub")
    rows, width = engagement.shape
    tiles = pattern.shape[0]
    assert n == nb * ns and ns == 2
    chunks = 6
    npairs = n * (n - 1) // 2
    block = (width, width)
    scratch = [
        pltpu.VMEM((rows, width), jnp.bfloat16),
        pltpu.VMEM((n, rows, width), jnp.bfloat16),
        pltpu.VMEM((npairs,) + block, jnp.float32),
        pltpu.VMEM((npairs,) + block, jnp.float32),
        pltpu.VMEM(block, jnp.float32),
        pltpu.VMEM((2 * nb,) + block, jnp.float32),
        pltpu.SemaphoreType.DMA,
        pltpu.SemaphoreType.DMA((2, chunks)),
        pltpu.SemaphoreType.DMA((n, chunks)),
        pltpu.SemaphoreType.DMA((npairs,)),
        pltpu.SemaphoreType.DMA((npairs,)),
        pltpu.SemaphoreType.DMA((npairs,)),
        pltpu.SemaphoreType.DMA((2 * nb,)),
        pltpu.SemaphoreType.DMA,
    ]
    vmem = pl.BlockSpec(memory_space=pltpu.VMEM)
    held = (n + 1) * rows * width * 2 + (2 * npairs + 2 * nb + 2) * width * width * 4
    return pl.pallas_call(
        functools.partial(kernel, n, nb, ns, chunks),
        out_shape=jax.ShapeDtypeStruct(block, jnp.float32),
        in_specs=[pl.BlockSpec(memory_space=pl.ANY), vmem, vmem],
        out_specs=vmem,
        scratch_shapes=scratch,
        compiler_params=pltpu.CompilerParams(
            collective_id=0, has_side_effects=True, vmem_limit_bytes=held + (12 << 20)
        ),
    )(engagement, pattern, degree.reshape(tiles, rows // tiles))


def solution(mesh):
    placed = (
        P(("grp", "blk", "sub"), "user"),
        P(("grp", "blk", "sub"), None),
        P(("grp", "blk", "sub")),
    )
    return jax.shard_map(
        on_device,
        mesh=mesh,
        in_specs=placed,
        out_specs=P(("grp", "user"), ("blk", "sub")),
        check_vma=False,
    )
```

time: 107 us -> 33.8 us (0.32)
  waiting for transfers between devices: 83.9 us -> 0 us
  Pallas kernels: 0 us -> 30.7 us
  between operations: 13.4 us -> 0.01 us
  other arithmetic: 5.09 us -> 0 us
  matrix products: 3.46 us -> 0 us
  local copies, waits for them, and re-layouts: 0.07 us -> 2.54 us
    all_gather x1 -> x0, waiting for transfers between devices: 65.7 us -> none  [on_device(): lax.all_gather(left, 'user', axis=1, tiled=True)]
    pallas_call x0 -> x1, Pallas kernels: none -> 30.7 us  [on_device(): pl.pallas_call(functools.partial(kernel, n, nb, ns, chunks), out_shape=ja...]
    reduce_scatter x1 -> x0, waiting for transfers between devices: 18.2 us -> none  [on_device(): lax.psum_scatter(partial_rows, ('blk', 'sub'), scatter_dimension=1, tiled...]
    convert_element_type x1 -> x0, other arithmetic: 3.67 us -> none  [on_device(): left = (masked.astype(jnp.float32) * weight[:, None]).astype(jnp.bfloat16)]
    dot_general x1 -> x0, matrix products: 3.46 us -> none  [contract(): lax.dot_general(first, second, (((0,), (0,)), ((), ())), preferred_elemen...]
    unnamed x0 -> x6, local copies, waits for them, and re-layouts: none -> 2.54 us
    mul x2 -> x0, other arithmetic: 1.41 us -> none  [the longest x1 0.72 us: on_device(): jnp.sqrt(lax.rsqrt(degree.astype(jnp.float32)))]
  transfers between devices with their start and end apart: 2 -> 0, of which waited for: 2 -> 0; matrix products, arithmetic and copies ran while one was open for 0% -> 0% of each run, Pallas kernels for 0% -> 0%
where the time goes in v1:
time: 33.8 us; the launch traced here: 33.3 us
  Pallas kernels  30.7 us (91%)
  local copies, waits for them, and re-layouts  2.54 us (8%)
    pallas_call x1, Pallas kernels, on_device(): pl.pallas_call(functools.partial(kernel, n, nb, ns, chunks), out_shape=ja...  30.7 us
    unnamed x6, local copies, waits for them, and re-layouts  2.54 us

profile of v1, /device:TPU:1, one launch (start us, length us, event | category | flops | bytes accessed | tf_op | source)
XLA Modules:
  0.0 33.3 jit_solution(8011734594621422342)
XLA Ops:
  0.0 0.0 copy-start.1
  0.0 0.8 %copy.4.pattern_ref = s32[24,4]{1,0:T(8,128)S(1)} copy(s32[24,4]{0,1:T(4,128)} %param.4) | data formatting | bytes 768 | tf_op args[1]
  0.8 0.0 copy-done.1
  0.8 0.0 copy-start
  0.8 1.1 %copy-done = bf16[3072,128]{1,0:T(8,128)(2,1)S(1)} copy-done((bf16[3072,128]{1,0:T(8,128)(2,1)S(1)}, bf16[3072,128]{1,0:T(8,128)(2,1)}, u32[]{:S(2)}) %copy-start) | copy-done | bytes 786456
  1.9 30.7 %shard_map.37 = f32[128,128]{1,0:T(8,128)S(1)} custom-call(bf16[3072,128]{1,0:T(8,128)(2,1)S(1)} %copy-done, s32[24,4]{1,0:T(8,128)S(1)} %copy.4.pattern_ref, s32[24,128]{1,0:T(8,128)S(1)} %bitcast.1), custom_call_target="tpu_custom_call" | custom-call | tf_op jit(solution)/shard_map/pallas_call | solution.py:250
  32.6 0.6 %copy.6 = f32[128,128]{1,0:T(8,128)} copy(f32[128,128]{1,0:T(8,128)S(1)} %shard_map.37) | data formatting | bytes 131072
Async XLA Ops:
  0.0 0.8 %copy-start.1 = (s32[3072]{0:T(1024)S(1)}, s32[3072]{0:T(1024)}, u32[]{:S(2)}) copy-start(s32[3072]{0:T(1024)} %param.5) | copy-start | bytes 36868
  0.8 1.1 %copy-start = (bf16[3072,128]{1,0:T(8,128)(2,1)S(1)}, bf16[3072,128]{1,0:T(8,128)(2,1)}, u32[]{:S(2)}) copy-start(bf16[3072,128]{1,0:T(8,128)(2,1)} %eng_hbm.1) | copy-start | bytes 2359300

commit v2 on v1

--- a/solution.py
+++ b/solution.py
@@ -34,32 +34,44 @@
     step = half // chunks
     procs = (n // 2 - 1, n // 2)
     column = x * ns + c
-    pairs = [(i, j) for i in range(n) for j in range(i + 1, n)]
-
-    load = pltpu.make_async_copy(eng_hbm, eng, load_sem)
-    load.start()
+    is_proc = (z == procs[0]) | (z == procs[1])
+
+    first = jnp.where((z < procs[0]) | (z == procs[1]), 0, 1)
+
+    def load(p):
+        at = pl.ds(pl.multiple_of(p * half, half), half)
+        return pltpu.make_async_copy(eng_hbm.at[at, :], eng.at[at, :], load_sem.at[p])
+
+    load(first).start()
+    load(1 - first).start()
 
     barrier = pltpu.get_barrier_semaphore()
-    everyone = n * nb * ns
-
-    def greet(k, carry):
-        zz, xx, cc = k // (nb * ns), (k // ns) % nb, k % ns
-
-        @pl.when((zz != z) | (xx != x) | (cc != c))
-        def _():
-            pl.semaphore_signal(barrier, inc=1, device_id=(g, zz, xx, cc), device_id_type=MESH)
-
-        return carry
-
-    lax.fori_loop(0, everyone, greet, 0)
-
-    lanes = lax.broadcasted_iota(jnp.int32, pattern_ref.shape, 1)
-    mask = jnp.sum(jnp.where(lanes == z, pattern_ref[...], 0), axis=1, keepdims=True)
+
+    def sends(source, target):
+        (sz, sx, sc), (tz, tx, tc) = source, target
+        source_proc = (sz == procs[0]) | (sz == procs[1])
+        target_proc = (tz == procs[0]) | (tz == procs[1])
+        block = target_proc & (sx == tx) & (sc == tc)
+        core = source_proc & (sz == tz) & (sx == tx)
+        pair = source_proc & (sc == tc) & (tz < tx * ns + tc)
+        own = (sz == tz) & (tz == tx * ns + tc)
+        same = (sz == tz) & (sx == tx) & (sc == tc)
+        return (block | core | pair | own) & jnp.logical_not(same)
+
+    def greet(k, count):
+        device = (k // (nb * ns), (k // ns) % nb, k % ns)
+
+        @pl.when(sends(device, (z, x, c)))
+        def _():
+            pl.semaphore_signal(barrier, inc=1, device_id=(g,) + device, device_id_type=MESH)
+
+        return count + jnp.where(sends((z, x, c), device), 1, 0)
+
+    targets = lax.fori_loop(0, n * nb * ns, greet, 0)
+
+    mask = pattern_ref[pl.ds(z, 1), :].astype(jnp.float32)
     weight = jnp.sqrt(lax.rsqrt(degree_ref[...].astype(jnp.float32)))
-    weight = weight * float(rows * nb * ns) ** (-0.25) * mask.astype(jnp.float32)
-    weight = weight.T
-
-    load.wait()
+    weight = (weight * float(rows * nb * ns) ** (-0.25)).T * mask
 
     def prepare(p, k):
         start = p * half + k * step
@@ -75,20 +87,29 @@
             dst_ref=left.at[source, at, :],
             send_sem=in_send.at[p, k],
             recv_sem=in_recv.at[source, k],
-            device_id=(g, procs[p] if isinstance(p, int) else procs[0] + p, x, c),
+            device_id=(g, procs[p], x, c),
             device_id_type=MESH,
         )
 
-    for k in range(chunks):
-        for p in range(2):
-            prepare(p, k)
-        if k == 0:
-            pl.semaphore_wait(barrier, everyone - 1)
-        for p in range(2):
-
-            @pl.when(z != procs[p])
-            def _():
-                block_copy(z, p, k).start()
+    def send_half(p, k, greeted):
+        prepare(p, k)
+        if not greeted:
+            pl.semaphore_wait(barrier, targets)
+
+        @pl.when(z != procs[p])
+        def _():
+            block_copy(z, p, k).start()
+
+    for p in range(2):
+
+        @pl.when(first == p)
+        def _():
+            load(p).wait()
+            for k in range(chunks):
+                send_half(p, k, k > 0)
+            load(1 - p).wait()
+            for k in range(chunks):
+                send_half(1 - p, k, True)
 
     def diag_copy(slot):
         return pltpu.make_async_remote_copy(
@@ -126,43 +147,51 @@
             device_id_type=MESH,
         )
 
-    is_proc = (z == procs[0]) | (z == procs[1])
-
-    @pl.when(is_proc)
-    def _():
-        p = z - procs[0]
-        acc[...] = jnp.zeros_like(acc)
+    def pairs_of(p, blocks, pairs):
+        for i, j in pairs:
+            s = pair_slot(n, i, j)
+            acc[s] = jnp.zeros_like(acc[s])
 
         def multiply(k, carry):
-            for i in range(n):
-
-                @pl.when(z != i)
-                def _():
-                    block_copy(i, p, k).wait_recv()
-
+            for i in blocks:
+                block_copy(i, p, k).wait_recv()
             at = pl.ds(pl.multiple_of(p * half + k * step, 16), step)
-            for s, (i, j) in enumerate(pairs):
-                acc[s] += contract(left[i, at, :], left[j, at, :])
+            for i, j in pairs:
+                acc[pair_slot(n, i, j)] += contract(left[i, at, :], left[j, at, :])
             return carry
 
         lax.fori_loop(0, chunks, multiply, 0)
 
-        for s, (i, j) in enumerate(pairs):
+        for i, j in pairs:
 
             @pl.when(c != j % ns)
             def _():
-                core_copy(s).start()
-
-        for s, (i, j) in enumerate(pairs):
+                core_copy(pair_slot(n, i, j)).start()
+
+        for i, j in pairs:
+            s = pair_slot(n, i, j)
 
             @pl.when(c == j % ns)
             def _():
                 core_copy(s).wait_recv()
                 acc[s] += other[s]
 
-                @pl.when((z != i) | (x != j // ns))
+                @pl.when((procs[p] != i) | (x != j // ns))
                 def _():
                     out_copy(s, p * nb + x, i, j).start()
+
+    pairs = [(i, j) for i in range(n) for j in range(i + 1, n)]
+    for p in range(2):
+
+        @pl.when(z == procs[p])
+        def _():
+            below, above = range(procs[0]), range(procs[1] + 1, n)
+            near, far = (below, above) if p == 0 else (above, below)
+            early = [pair for pair in pairs if not set(pair) & set(far)]
+            late = sorted((pair for pair in pairs if set(pair) & set(far)), key=lambda pair: abs(pair[0] - procs[p]), reverse=True)
+            pairs_of(p, [*near, procs[1 - p]], early)
+            if late:
+                pairs_of(p, far, late)
 
     @pl.when(column < z)
     def _():
@@ -226,7 +255,7 @@
     rows, width = engagement.shape
     tiles = pattern.shape[0]
     assert n == nb * ns and ns == 2
-    chunks = 6
+    chunks = 4
     npairs = n * (n - 1) // 2
     block = (width, width)
     scratch = [
@@ -236,7 +265,7 @@
         pltpu.VMEM((npairs,) + block, jnp.float32),
         pltpu.VMEM(block, jnp.float32),
         pltpu.VMEM((2 * nb,) + block, jnp.float32),
-        pltpu.SemaphoreType.DMA,
+        pltpu.SemaphoreType.DMA((2,)),
         pltpu.SemaphoreType.DMA((2, chunks)),
         pltpu.SemaphoreType.DMA((n, chunks)),
         pltpu.SemaphoreType.DMA((npairs,)),
@@ -246,7 +275,6 @@
         pltpu.SemaphoreType.DMA,
     ]
     vmem = pl.BlockSpec(memory_space=pltpu.VMEM)
-    held = (n + 1) * rows * width * 2 + (2 * npairs + 2 * nb + 2) * width * width * 4
     return pl.pallas_call(
         functools.partial(kernel, n, nb, ns, chunks),
         out_shape=jax.ShapeDtypeStruct(block, jnp.float32),
@@ -254,9 +282,9 @@
         out_specs=vmem,
         scratch_shapes=scratch,
         compiler_params=pltpu.CompilerParams(
-            collective_id=0, has_side_effects=True, vmem_limit_bytes=held + (12 << 20)
+            collective_id=0, has_side_effects=True, vmem_limit_bytes=60 << 20
         ),
-    )(engagement, pattern, degree.reshape(tiles, rows // tiles))
+    )(engagement, pattern.T, degree.reshape(tiles, rows // tiles))
 
 
 def solution(mesh):

time: 33.8 us -> 31.4 us (0.929)
  local copies, waits for them, and re-layouts: 2.54 us -> 1.47 us
  Pallas kernels: 30.7 us -> 29.7 us
    unnamed x6 -> x1, local copies, waits for them, and re-layouts: 2.54 us -> 1.47 us
    pallas_call x1, Pallas kernels: 30.7 us -> 29.7 us  [on_device(): pl.pallas_call(functools.partial(kernel, n, nb, ns, chunks), out_shape=ja...]
where the time goes in v2:
time: 31.4 us; the launch traced here: 31.1 us
  Pallas kernels  29.7 us (95%)
  local copies, waits for them, and re-layouts  1.47 us (5%)
    pallas_call x1, Pallas kernels, on_device(): pl.pallas_call(functools.partial(kernel, n, nb, ns, chunks), out_shape=ja...  29.7 us
    unnamed x1, local copies, waits for them, and re-layouts  1.47 us

profile of v2, /device:TPU:1, one launch (start us, length us, event | category | flops | bytes accessed | tf_op | source)
XLA Modules:
  0.0 31.1 jit_solution(1051947180460043648)
XLA Ops:
  0.0 29.7 %shard_map.37 = f32[128,128]{1,0:T(8,128)} custom-call(bf16[3072,128]{1,0:T(8,128)(2,1)} %eng_hbm.1, s32[4,24]{1,0:T(4,128)} %bitcast.3, s32[24,128]{1,0:T(8,128)} %bitcast.2), custom_call_target="tpu_custom_call" | custom-call | tf_op jit(solution)/shard_map/pallas_call | solution.py:278
  29.7 1.5 %copy.5 = f32[128,128]{1,0:T(8,128)} copy(f32[128,128]{1,0:T(8,128)} %shard_map.37) | data formatting | bytes 131072

commit v3 on v2

--- a/solution.py
+++ b/solution.py
@@ -38,12 +38,13 @@
 
     first = jnp.where((z < procs[0]) | (z == procs[1]), 0, 1)
 
-    def load(p):
-        at = pl.ds(pl.multiple_of(p * half, half), half)
-        return pltpu.make_async_copy(eng_hbm.at[at, :], eng.at[at, :], load_sem.at[p])
-
-    load(first).start()
-    load(1 - first).start()
+    def load(p, k):
+        at = pl.ds(pl.multiple_of(p * half + k * step, step), step)
+        return pltpu.make_async_copy(eng_hbm.at[at, :], eng.at[at, :], load_sem.at[p, k])
+
+    for p in (first, 1 - first):
+        for k in range(chunks):
+            load(p, k).start()
 
     barrier = pltpu.get_barrier_semaphore()
 
@@ -92,6 +93,7 @@
         )
 
     def send_half(p, k, greeted):
+        load(p, k).wait()
         prepare(p, k)
         if not greeted:
             pl.semaphore_wait(barrier, targets)
@@ -104,10 +106,8 @@
 
         @pl.when(first == p)
         def _():
-            load(p).wait()
             for k in range(chunks):
                 send_half(p, k, k > 0)
-            load(1 - p).wait()
             for k in range(chunks):
                 send_half(1 - p, k, True)
 
@@ -255,7 +255,7 @@
     rows, width = engagement.shape
     tiles = pattern.shape[0]
     assert n == nb * ns and ns == 2
-    chunks = 4
+    chunks = 3
     npairs = n * (n - 1) // 2
     block = (width, width)
     scratch = [
@@ -265,7 +265,7 @@
         pltpu.VMEM((npairs,) + block, jnp.float32),
         pltpu.VMEM(block, jnp.float32),
         pltpu.VMEM((2 * nb,) + block, jnp.float32),
-        pltpu.SemaphoreType.DMA((2,)),
+        pltpu.SemaphoreType.DMA((2, chunks)),
         pltpu.SemaphoreType.DMA((2, chunks)),
         pltpu.SemaphoreType.DMA((n, chunks)),
         pltpu.SemaphoreType.DMA((npairs,)),
@@ -275,16 +275,18 @@
         pltpu.SemaphoreType.DMA,
     ]
     vmem = pl.BlockSpec(memory_space=pltpu.VMEM)
-    return pl.pallas_call(
+    result = pl.pallas_call(
         functools.partial(kernel, n, nb, ns, chunks),
         out_shape=jax.ShapeDtypeStruct(block, jnp.float32),
         in_specs=[pl.BlockSpec(memory_space=pl.ANY), vmem, vmem],
         out_specs=vmem,
         scratch_shapes=scratch,
         compiler_params=pltpu.CompilerParams(
-            collective_id=0, has_side_effects=True, vmem_limit_bytes=60 << 20
+            collective_id=0, has_side_effects=True, vmem_limit_bytes=58 << 20
         ),
     )(engagement, pattern.T, degree.reshape(tiles, rows // tiles))
+    column = lax.axis_index("blk") * ns + lax.axis_index("sub")
+    return jnp.where(column >= lax.axis_index("user"), result, jnp.float32(0.0))
 
 
 def solution(mesh):

time: 31.4 us -> 31.4 us (level)
  other arithmetic: 0 us -> 1.49 us
  local copies, waits for them, and re-layouts: 1.47 us -> 0 us
    select_n x0 -> x1, other arithmetic: none -> 1.49 us  [on_device(): return jnp.where(column >= lax.axis_index('user'), result, jnp.float32(0.0))]
    unnamed x1 -> x0, local copies, waits for them, and re-layouts: 1.47 us -> none
where the time goes in v3:
time: 31.4 us; the launch traced here: 31.2 us
  Pallas kernels  29.7 us (95%)
  other arithmetic  1.49 us (5%)
    pallas_call x1, Pallas kernels, on_device(): pl.pallas_call(functools.partial(kernel, n, nb, ns, chunks), out_shape=ja...  29.7 us
    select_n x1, other arithmetic, on_device(): return jnp.where(column >= lax.axis_index('user'), result, jnp.float32(0.0))  1.49 us

profile of v3, /device:TPU:1, one launch (start us, length us, event | category | flops | bytes accessed | tf_op | source)
XLA Modules:
  0.0 31.2 jit_solution(1955868862474043255)
XLA Ops:
  0.0 29.7 %shard_map.37 = f32[128,128]{1,0:T(8,128)} custom-call(bf16[3072,128]{1,0:T(8,128)(2,1)} %eng_hbm.1, s32[4,24]{1,0:T(4,128)} %bitcast.3, s32[24,128]{1,0:T(8,128)} %bitcast.2), custom_call_target="tpu_custom_call" | custom-call | tf_op jit(solution)/shard_map/pallas_call | solution.py:278
  29.7 1.5 %broadcast_select_fusion = f32[128,128]{1,0:T(8,128)} fusion(f32[128,128]{1,0:T(8,128)} %shard_map.37, pred[]{:T(512)S(6)} %ge.3), kind=kLoop, calls=%fused_computation | loop fusion | flops 16384 | bytes 131073 | tf_op jit(solution)/shard_map/jit(_where)/select_n | solution.py:289
